TPU v7x, 32 devices: a whole 2x2x4 slice. The times are simulated.
32 devices in a mesh: rep: 2 (over x), gx: 4 (over y, core), gy: 4 (over z).
Axes of the slice: x: 2, y: 2, z: 4, core: 2. Of those that a mesh axis runs over, the one named last changes fastest.
Arguments:
- tokens: bfloat16 [4096, 2048], P(('rep', 'gx', 'gy')), parts along dimension 0, may hold values from -6 to 6
- grad_out: bfloat16 [4096, 2048], P(('rep', 'gx', 'gy')), parts along dimension 0, may hold values from -6 to 6
- route_ids: int32 [4096, 10], P(('rep', 'gx', 'gy')), parts along dimension 0, may hold values from 0 to 31, all different within a row; in each aligned block of 128 rows (0 to 127, 128 to 255, ...) at most 50 rows name the same one
- gate_weights: float32 [4096, 10], P(('rep', 'gx', 'gy')), parts along dimension 0, may hold values from 0.05 to 0.5
- w_gate: bfloat16 [32, 2048, 256], P(('gx', 'gy')), may hold values from -0.125 to 0.125
- w_up: bfloat16 [32, 2048, 256], P(('gx', 'gy')), may hold values from -0.125 to 0.125
- w_down: bfloat16 [32, 256, 2048], P(('gx', 'gy')), may hold values from -0.375 to 0.375
Outputs:
- grad_tokens: bfloat16 [4096, 2048], P(('rep', 'gx', 'gy')), parts along dimension 0
- grad_down: bfloat16 [64, 256, 2048], P(('rep', 'gx', 'gy')), parts along dimension 0
There are 2 independent parts, one for each index of `rep`. A program takes and returns all parts, laid end to end along the dimension named above; an argument that names none is the same for every part. Nothing has to cross between parts.
Inputs may be any that keep to these rules, and one draw needn't show every extreme that they name: `route_ids`: each row names 10 different experts. Among the 128 rows of one device no expert is named by more than 50 rows, and in some aligned block of 128 rows some expert is named by exactly 50 rows.
All inputs are finite; a program needn't handle non-finite values.
Results may differ from a plain program's by a relative error of at most 0.0064.
Values may be sent and summed in bfloat16 or wider, within the bound.
A program may use at most 128 MiB of HBM per device.

v0:
```python
import jax
import jax.numpy as jnp
from jax import lax
from jax.sharding import PartitionSpec as P


def shards(tokens, grad_out, route_ids, gate_weights, w_gate, w_up, w_down):
    token_count = tokens.shape[0]
    model_width = tokens.shape[1]
    fanout = route_ids.shape[1]
    local_experts = w_gate.shape[0]
    outer_size = lax.axis_size("gx")
    inner_size = lax.axis_size("gy")
    devices = outer_size * inner_size
    experts = local_experts * devices
    capacity = max(2, 5 * token_count * fanout // (4 * experts))
    flat_ids = route_ids.reshape(-1)
    onehot = (flat_ids[:, None] == jnp.arange(experts, dtype=jnp.int32)[None, :]).astype(jnp.int32)
    earlier = jnp.cumsum(onehot, axis=0) - onehot
    slot_index = jnp.sum(earlier * onehot, axis=1)
    target = flat_ids // local_experts
    within = flat_ids % local_experts
    position = (within * devices + target) * capacity + slot_index
    source_rows = jnp.repeat(tokens, fanout, axis=0)
    scaled = (gate_weights.reshape(-1, 1) * jnp.repeat(grad_out, fanout, axis=0)).astype(
        jnp.bfloat16
    )
    buffer_rows = local_experts * devices * capacity
    send_inputs = jnp.zeros((buffer_rows, model_width), jnp.bfloat16).at[position].set(source_rows)
    send_grads = jnp.zeros((buffer_rows, model_width), jnp.bfloat16).at[position].set(scaled)
    flat_shape = (local_experts, devices, capacity, model_width)
    got_inputs, got_grads = (
        lax.all_to_all(
            send_inputs.reshape(flat_shape), ("gx", "gy"), split_axis=1, concat_axis=1, tiled=True
        ),
        lax.all_to_all(
            send_grads.reshape(flat_shape), ("gx", "gy"), split_axis=1, concat_axis=1, tiled=True
        ),
    )
    expert_rows = devices * capacity
    inputs = got_inputs.reshape(local_experts, expert_rows, model_width)
    routed = got_grads.reshape(local_experts, expert_rows, model_width)
    pre_gate = jnp.einsum("emd,edf->emf", inputs, w_gate, preferred_element_type=jnp.float32)
    pre_up = jnp.einsum("emd,edf->emf", inputs, w_up, preferred_element_type=jnp.float32)
    sigma = jax.nn.sigmoid(pre_gate)
    silu_val = pre_gate * sigma
    hidden = (silu_val * pre_up).astype(jnp.bfloat16)
    grad_hidden = jnp.einsum("emd,efd->emf", routed, w_down, preferred_element_type=jnp.float32)
    grad_first = (grad_hidden * pre_up * sigma * (1.0 + pre_gate * (1.0 - sigma))).astype(
        jnp.bfloat16
    )
    grad_second = (grad_hidden * silu_val).astype(jnp.bfloat16)
    grad_route = (
        jnp.einsum("emf,edf->emd", grad_first, w_gate, preferred_element_type=jnp.float32)
        + jnp.einsum("emf,edf->emd", grad_second, w_up, preferred_element_type=jnp.float32)
    ).astype(jnp.bfloat16)
    grad_down = jnp.einsum(
        "emf,emd->efd", hidden, routed, preferred_element_type=jnp.float32
    ).astype(jnp.bfloat16)
    returned = lax.all_to_all(
        grad_route.reshape(flat_shape), ("gx", "gy"), split_axis=1, concat_axis=1, tiled=True
    )
    picked = returned.reshape(buffer_rows, model_width)[position]
    grad_tokens = jnp.sum(
        picked.astype(jnp.float32).reshape(token_count, fanout, model_width), axis=1
    ).astype(jnp.bfloat16)
    return (grad_tokens, grad_down)


def solution(mesh):
    placed = (
        P(("rep", "gx", "gy"), None),
        P(("rep", "gx", "gy"), None),
        P(("rep", "gx", "gy"), None),
        P(("rep", "gx", "gy"), None),
        P(("gx", "gy"), None, None),
        P(("gx", "gy"), None, None),
        P(("gx", "gy"), None, None),
    )
    return jax.shard_map(
        shards,
        mesh=mesh,
        in_specs=placed,
        out_specs=(P(("rep", "gx", "gy"), None), P(("rep", "gx", "gy"), None, None)),
        check_vma=False,
    )
```

profile of v0, /device:TPU:0, one launch (start us, length us, event | category | flops | bytes accessed | tf_op | source)
XLA Modules:
  0.0 647.3 jit_solution(5697402835497428527)
XLA Ops:
  0.6 0.9 copy.23
  2.0 9.1 %reduce-window.6 = s32[32,10,128]{2,1,0:T(8,128)S(1)} reduce-window(s32[32,10,128]{2,1,0:T(8,128)S(1)} %fusion.21, s32[]{:T(128)} %constant.36.clone.1), window={size=1x1x128 pad=0_0x0_0x127_0}, to_apply=%region_0.0 | reduce-window | flops 5201920 | bytes 327684 | tf_op jit(solution)/shard_map/reduce-window
  11.3 0.2 copy.26
  11.7 5.4 broadcast_in_dim.5
  17.1 9.8 %reshape.200 = bf16[1280,2048]{1,0:T(8,128)(2,1)} reshape(bf16[128,10,2048]{2,1,0:T(8,128)(2,1)} %broadcast_in_dim.5) | data formatting | bytes 10485760 | tf_op jit(solution)/shard_map/reshape | solution.py:24
  27.1 14.8 %scatter_custom_fusion.1 = bf16[1600,2048]{1,0:T(8,128)(2,1)} fusion(s32[1280]{0:T(1024)S(1)} %fusion.25, bf16[1280,2048]{1,0:T(8,128)(2,1)} %reshape.200, bf16[]{:T(256)} %constant.35.clone.1), kind=kCustom, calls=%fused_computation.15 | custom fusion | bytes 6554112 | tf_op jit(solution)/shard_map/scatter | solution.py:29
  41.9 8.7 %reshape.176 = bf16[2,16,50,2048]{3,2,1,0:T(8,128)(2,1)} reshape(bf16[1600,2048]{1,0:T(8,128)(2,1)} %scatter_custom_fusion.1) | data formatting | bytes 13107200 | tf_op jit(solution)/shard_map/reshape | solution.py:34
  50.6 24.7 %copy.31 = bf16[2,16,50,2048]{3,0,2,1:T(2,128)(2,1)} copy(bf16[2,16,50,2048]{3,2,1,0:T(8,128)(2,1)} %reshape.176) | data formatting | bytes 13107200 | tf_op jit(solution)/shard_map/reshape | solution.py:34
  75.3 7.8 %all-to-all-start.1 = ((bf16[2,16,50,2048]{3,0,2,1:T(2,128)(2,1)}), bf16[2,16,50,2048]{3,0,2,1:T(2,128)(2,1)}, u32[]{:S(2)}, u32[]{:S(2)}) async-start(bf16[2,16,50,2048]{3,0,2,1:T(2,128)(2,1)} %copy.31), calls=%async_computation.1 | async-start | bytes 13107200 | tf_op jit(solution)/shard_map/all_to_all | solution.py:33
  83.4 7.9 %broadcast_in_dim.4 = f32[128,10,2048]{2,1,0:T(8,128)} broadcast(bf16[128,2048]{1,0:T(8,128)(2,1)S(1)} %copy-done.7), dimensions={0,2} | broadcast | bytes 11010048 | tf_op jit(solution)/shard_map/broadcast_in_dim | solution.py:25
  91.3 13.9 %convert_element_type.38 = f32[1280,2048]{1,0:T(8,128)} reshape(f32[128,10,2048]{2,1,0:T(8,128)} %broadcast_in_dim.4) | data formatting | bytes 20971520 | tf_op jit(solution)/shard_map/convert_element_type | solution.py:25
  105.2 20.5 %scatter_custom_fusion = bf16[1600,2048]{1,0:T(8,128)(2,1)} fusion(s32[1280]{0:T(1024)S(1)} %fusion.25, f32[1280,2048]{1,0:T(8,128)} %convert_element_type.38, f32[1280]{0:T(1024)S(1)} %mul.65, bf16[]{:T(256)} %constant.35.clone.1), kind=kCustom, calls=%fused_computation.13 | custom fusion | flops 5242880 | bytes 17047554 | tf_op jit(solution)/shard_map/scatter | solution.py:30
  125.7 8.7 %reshape.173 = bf16[2,16,50,2048]{3,2,1,0:T(8,128)(2,1)} reshape(bf16[1600,2048]{1,0:T(8,128)(2,1)} %scatter_custom_fusion) | data formatting | bytes 13107200 | tf_op jit(solution)/shard_map/reshape | solution.py:37
  134.4 24.8 %copy.29 = bf16[2,16,50,2048]{3,0,2,1:T(2,128)(2,1)} copy(bf16[2,16,50,2048]{3,2,1,0:T(8,128)(2,1)} %reshape.173) | data formatting | bytes 13107200 | tf_op jit(solution)/shard_map/reshape | solution.py:37
  159.1 69.0 %all-to-all-done.1 = bf16[2,16,50,2048]{3,0,2,1:T(2,128)(2,1)} async-done(((bf16[2,16,50,2048]{3,0,2,1:T(2,128)(2,1)}), bf16[2,16,50,2048]{3,0,2,1:T(2,128)(2,1)}, u32[]{:S(2)}, u32[]{:S(2)}) %all-to-all-start.1) | async-done | bytes 6553632 | tf_op jit(solution)/shard_map/all_to_all | solution.py:33
  228.1 14.4 %all-to-all-start = ((bf16[2,16,50,2048]{3,0,2,1:T(2,128)(2,1)}), bf16[2,16,50,2048]{3,0,2,1:T(2,128)(2,1)}, u32[]{:S(2)}, u32[]{:S(2)}) async-start(bf16[2,16,50,2048]{3,0,2,1:T(2,128)(2,1)} %copy.29), calls=%async_computation | async-start | bytes 13107200 | tf_op jit(solution)/shard_map/all_to_all | solution.py:36
  242.6 6.2 fusion
  248.8 6.0 fusion.2
  254.8 132.7 %all-to-all-done = bf16[2,16,50,2048]{3,0,2,1:T(2,128)(2,1)} async-done(((bf16[2,16,50,2048]{3,0,2,1:T(2,128)(2,1)}), bf16[2,16,50,2048]{3,0,2,1:T(2,128)(2,1)}, u32[]{:S(2)}, u32[]{:S(2)}) %all-to-all-start) | async-done | bytes 6553632 | tf_op jit(solution)/shard_map/all_to_all | solution.py:36
  387.5 5.8 fusion.6
  393.3 1.2 copy-done.4
  394.5 6.8 %fusion.17 = f32[2,800,2048]{2,1,0:T(8,128)} fusion(bf16[2,2048,256]{2,1,0:T(8,128)(2,1)S(1)} %copy-done, f32[2,800,256]{2,1,0:T(8,128)S(1)} %copy-done.2, f32[2,800,256]{2,1,0:T(8,128)S(1)} %fusion.6, f32[2,800,256]{2,1,0:T(8,128)S(1)} %copy-done.6), kind=kOutput, calls=%fused_computation.24 | convolution fusion | flops 1681817600 | bytes 20119552 | tf_op jit(solution)/shard_map/emf,edf->emd/dot_general | solution.py:54
  401.3 8.3 %add_convert_fusion = bf16[2,800,2048]{2,1,0:T(8,128)(2,1)S(1)} fusion(f32[2,800,2048]{2,1,0:T(8,128)} %fusion.17, bf16[2,2048,256]{2,1,0:T(8,128)(2,1)} %param.12, f32[2,800,256]{2,1,0:T(8,128)} %copy-done.4, f32[2,800,256]{2,1,0:T(8,128)} %fusion), kind=kOutput, calls=%fused_computation.3 | convolution fusion | flops 1686732800 | bytes 25034752 | tf_op jit(solution)/shard_map/emf,edf->emd/dot_general | solution.py:55
  409.6 36.6 %copy.34 = bf16[2,800,2048]{2,0,1:T(2,128)(2,1)} copy(bf16[2,800,2048]{2,1,0:T(8,128)(2,1)S(1)} %add_convert_fusion) | data formatting | bytes 13107200 | tf_op jit(solution)/shard_map/convert_element_type | solution.py:56
  446.2 5.0 all-to-all-start.2
  451.3 9.6 %fusion.13 = bf16[2,256,2048]{2,1,0:T(8,128)(2,1)} fusion(bf16[2,800,2048]{2,0,1:T(2,128)(2,1)} %bitcast.2, f32[2,800,256]{2,1,0:T(8,128)} %fusion.2, f32[2,800,256]{2,1,0:T(8,128)S(1)} %copy-done.3), kind=kOutput, calls=%fused_computation.18 | convolution fusion | flops 1681227776 | bytes 11927552 | tf_op jit(solution)/shard_map/emf,emd->efd/dot_general | solution.py:57
  460.9 135.3 %all-to-all-done.2 = bf16[2,16,50,2048]{3,0,2,1:T(2,128)(2,1)} async-done(((bf16[2,16,50,2048]{3,0,2,1:T(2,128)(2,1)}), bf16[2,16,50,2048]{3,0,2,1:T(2,128)(2,1)}, u32[]{:S(2)}, u32[]{:S(2)}) %all-to-all-start.2) | async-done | bytes 6553632 | tf_op jit(solution)/shard_map/all_to_all | solution.py:60
  596.2 9.1 %copy.35 = bf16[2,16,50,2048]{3,2,1,0:T(8,128)(2,1)} copy(bf16[2,16,50,2048]{3,0,2,1:T(2,128)(2,1)} %all-to-all-done.2) | data formatting | bytes 13107200 | tf_op jit(solution)/shard_map/all_to_all | solution.py:60
  605.2 8.8 %reshape.179 = bf16[1600,2048]{1,0:T(8,128)(2,1)} reshape(bf16[2,16,50,2048]{3,2,1,0:T(8,128)(2,1)} %copy.35) | data formatting | bytes 13107200 | tf_op jit(solution)/shard_map/reshape | solution.py:63
  614.0 14.5 %gather_fusion = bf16[1280,2048]{1,0:T(8,128)(2,1)} fusion(bf16[1600,2048]{1,0:T(8,128)(2,1)} %reshape.179, s32[2048]{0:T(1024)S(1)} %pad_clamp_fusion), kind=kCustom, calls=%fused_computation | custom fusion | bytes 10490880 | tf_op jit(solution)/shard_map/gather | solution.py:63
  628.6 9.9 %gather.6 = bf16[128,10,2048]{2,1,0:T(8,128)(2,1)} reshape(bf16[1280,2048]{1,0:T(8,128)(2,1)} %gather_fusion) | data formatting | bytes 10485760 | tf_op jit(solution)/shard_map/gather | solution.py:63
  638.5 8.3 %reduce_sum.25 = bf16[128,2048]{1,0:T(8,128)(2,1)} reduce(bf16[128,10,2048]{2,1,0:T(8,128)(2,1)} %gather.6, bf16[]{:T(256)} %constant.35.clone.1), dimensions={1}, to_apply=%region_5.6 | reduce | flops 2359296 | bytes 5767170 | tf_op jit(solution)/shard_map/reduce_sum | solution.py:64
  (30 shorter events, 1.2 us)
Async XLA Ops:
  0.6 241.9 %copy-start = (bf16[2,2048,256]{2,1,0:T(8,128)(2,1)S(1)}, bf16[2,2048,256]{2,1,0:T(8,128)(2,1)}, u32[]{:S(2)}) copy-start(bf16[2,2048,256]{2,1,0:T(8,128)(2,1)} %param.11) | copy-start | bytes 6291460
  75.3 7.8 %copy-start.8 = (f32[128,10]{0,1:T(8,128)S(1)}, f32[128,10]{0,1:T(8,128)}, u32[]{:S(2)}) copy-start(f32[128,10]{0,1:T(8,128)} %param.10) | copy-start | bytes 15364
  75.3 8.1 %copy-start.7 = (bf16[128,2048]{1,0:T(8,128)(2,1)S(1)}, bf16[128,2048]{1,0:T(8,128)(2,1)}, u32[]{:S(2)}) copy-start(bf16[128,2048]{1,0:T(8,128)(2,1)} %param.8) | copy-start | bytes 1572868
  75.3 152.8 %all-to-all-start.1 = ((bf16[2,16,50,2048]{3,0,2,1:T(2,128)(2,1)}), bf16[2,16,50,2048]{3,0,2,1:T(2,128)(2,1)}, u32[]{:S(2)}, u32[]{:S(2)}) async-start(bf16[2,16,50,2048]{3,0,2,1:T(2,128)(2,1)} %copy.31), calls=%async_computation.1 | async-start | bytes 13107200 | tf_op jit(solution)/shard_map/all_to_all | solution.py:33
  228.1 159.4 %all-to-all-start = ((bf16[2,16,50,2048]{3,0,2,1:T(2,128)(2,1)}), bf16[2,16,50,2048]{3,0,2,1:T(2,128)(2,1)}, u32[]{:S(2)}, u32[]{:S(2)}) async-start(bf16[2,16,50,2048]{3,0,2,1:T(2,128)(2,1)} %copy.29), calls=%async_computation | async-start | bytes 13107200 | tf_op jit(solution)/shard_map/all_to_all | solution.py:36
  242.6 6.2 copy-start.5
  387.5 7.0 %copy-start.2 = (f32[2,800,256]{2,1,0:T(8,128)S(1)}, f32[2,800,256]{2,1,0:T(8,128)}, u32[]{:S(2)}) copy-start(f32[2,800,256]{2,1,0:T(8,128)} %fusion) | copy-start | bytes 4915204
  387.5 7.0 %copy-start.6 = (f32[2,800,256]{2,1,0:T(8,128)S(1)}, f32[2,800,256]{2,1,0:T(8,128)}, u32[]{:S(2)}) copy-start(f32[2,800,256]{2,1,0:T(8,128)} %fusion.2) | copy-start | bytes 4915204
  393.3 1.2 copy-start.4
  446.2 5.0 copy-start.3
  446.2 149.9 %all-to-all-start.2 = ((bf16[2,16,50,2048]{3,0,2,1:T(2,128)(2,1)}), bf16[2,16,50,2048]{3,0,2,1:T(2,128)(2,1)}, u32[]{:S(2)}, u32[]{:S(2)}) async-start(bf16[2,16,50,2048]{3,0,2,1:T(2,128)(2,1)} %bitcast.29), calls=%async_computation.2 | async-start | bytes 13107200 | tf_op jit(solution)/shard_map/all_to_all | solution.py:60
  628.6 18.3 %copy-start.1 = (bf16[2,2048,256]{2,1,0:T(8,128)(2,1)S(1)}, bf16[2,2048,256]{2,1,0:T(8,128)(2,1)}, u32[]{:S(2)}) copy-start(bf16[2,2048,256]{2,1,0:T(8,128)(2,1)} %param.11) | copy-start | bytes 6291460
where the time goes:
time: 657 us; the launch traced here: 647 us
  waiting for transfers between devices  337 us (51%)
  local copies, waits for them, and re-layouts  201 us (31%)
  matrix products  42.7 us (6%)
  other arithmetic  38.3 us (6%)
  starting transfers between devices  27.3 us (4%)
    all_to_all x1, waiting for transfers between devices, shards(): lax.all_to_all(grad_route.reshape(flat_shape), ('gx', 'gy'), split_axis=1...  135 us
    all_to_all x1, waiting for transfers between devices, shards(): lax.all_to_all(send_grads.reshape(flat_shape), ('gx', 'gy'), split_axis=1...  133 us
    all_to_all x1, waiting for transfers between devices, shards(): lax.all_to_all(send_inputs.reshape(flat_shape), ('gx', 'gy'), split_axis=...  69 us
    convert_element_type x1, local copies, waits for them, and re-layouts, shards(): grad_route = (jnp.einsum('emf,edf->emd', grad_first, w_gate, preferred_el...  36.6 us
    reshape x2, local copies, waits for them, and re-layouts, shards(): send_grads.reshape(flat_shape)  33.4 us
    reshape x2, local copies, waits for them, and re-layouts, shards(): send_inputs.reshape(flat_shape)  33.4 us
    gather x2, local copies, waits for them, and re-layouts, shards(): picked = returned.reshape(buffer_rows, model_width)[position]  24.5 us
    scatter x1, other arithmetic, shards(): jnp.zeros((buffer_rows, model_width), jnp.bfloat16).at[position].set(scaled)  20.5 us
  transfers between devices with their start and end apart: 3, of which 3 were waited for; matrix products, arithmetic and copies ran while one was open for 15% of the time, Pallas kernels for 0%

commit v1 on v0

--- a/solution.py
+++ b/solution.py
@@ -4,7 +4,7 @@
 from jax.sharding import PartitionSpec as P
 
 
-def shards(tokens, grad_out, route_ids, gate_weights, w_gate, w_up, w_down):
+def routed_shards(tokens, grad_out, route_ids, gate_weights, w_gate, w_up, w_down):
     token_count = tokens.shape[0]
     model_width = tokens.shape[1]
     fanout = route_ids.shape[1]
@@ -67,6 +67,53 @@
     return (grad_tokens, grad_down)
 
 
+def gathered_shards(tokens, grad_out, route_ids, gate_weights, w_gate, w_up, w_down):
+    axes = ("gx", "gy")
+    local_experts = w_gate.shape[0]
+    devices = lax.axis_size("gx") * lax.axis_size("gy")
+    experts = local_experts * devices
+    chosen = route_ids[:, :, None] == jnp.arange(experts, dtype=jnp.int32)
+    dense = jnp.sum(jnp.where(chosen, gate_weights[:, :, None], 0.0), axis=1)
+    all_gates = lax.all_gather(dense, axes, axis=0, tiled=True)
+    inputs = lax.all_gather(tokens, axes, axis=0, tiled=True)
+    grads = lax.all_gather(grad_out, axes, axis=0, tiled=True)
+    me = lax.axis_index("gx") * lax.axis_size("gy") + lax.axis_index("gy")
+    gates = lax.dynamic_slice_in_dim(all_gates, me * local_experts, local_experts, axis=1)
+    total = 0.0
+    downs = []
+    for e in range(local_experts):
+        routed = (gates[:, e : e + 1] * grads).astype(jnp.bfloat16)
+        pre_gate = jnp.dot(inputs, w_gate[e], preferred_element_type=jnp.float32)
+        pre_up = jnp.dot(inputs, w_up[e], preferred_element_type=jnp.float32)
+        sigma = jax.nn.sigmoid(pre_gate)
+        silu_val = pre_gate * sigma
+        hidden = (silu_val * pre_up).astype(jnp.bfloat16)
+        grad_hidden = jnp.dot(routed, w_down[e].T, preferred_element_type=jnp.float32)
+        first = grad_hidden * pre_up * sigma * (1.0 + pre_gate * (1.0 - sigma))
+        second = grad_hidden * silu_val
+        total = total + jnp.dot(
+            first.astype(jnp.bfloat16), w_gate[e].T, preferred_element_type=jnp.float32
+        )
+        total = total + jnp.dot(
+            second.astype(jnp.bfloat16), w_up[e].T, preferred_element_type=jnp.float32
+        )
+        downs.append(
+            jnp.dot(hidden.T, routed, preferred_element_type=jnp.float32).astype(jnp.bfloat16)
+        )
+    grad_tokens = lax.psum_scatter(
+        total.astype(jnp.bfloat16), axes, scatter_dimension=0, tiled=True
+    )
+    return (grad_tokens, jnp.stack(downs))
+
+
+def shards(*args):
+    route_ids, w_gate = args[2], args[4]
+    experts = w_gate.shape[0] * lax.axis_size("gx") * lax.axis_size("gy")
+    if experts <= 4 * route_ids.shape[1]:
+        return gathered_shards(*args)
+    return routed_shards(*args)
+
+
 def solution(mesh):
     placed = (
         P(("rep", "gx", "gy"), None),

time: 657 us -> 346 us (0.53); the launches traced: 647 us -> 346 us
  local copies, waits for them, and re-layouts: 201 us -> 1.38 us
  waiting for transfers between devices: 337 us -> 201 us
  matrix products: 42.7 us -> 87.6 us
  blocking collectives: 0 us -> 39.1 us
  other arithmetic: 38.3 us -> 2.24 us
  starting transfers between devices: 27.3 us -> 0.11 us
  between operations: 1.24 us -> 14 us
    all_to_all x3 -> x0, waiting for transfers between devices: 337 us -> none  [the longest x1 135 us: shards(): lax.all_to_all(grad_route.reshape(flat_shape), ('gx', 'gy'), split_axis=1...]
    all_gather x0 -> x2, waiting for transfers between devices: none -> 112 us  [the longest x1 69.4 us: gathered_shards(): grads = lax.all_gather(grad_out, axes, axis=0, tiled=True)]
    reduce_scatter x0 -> x1, waiting for transfers between devices: none -> 87.6 us  [gathered_shards(): lax.psum_scatter(total.astype(jnp.bfloat16), axes, scatter_dimension=0, t...]
    reshape x7 -> x0, local copies, waits for them, and re-layouts: 85.6 us -> none  [the longest x2 33.4 us: shards(): send_grads.reshape(flat_shape)]
    convert_element_type x2 -> x0, local copies, waits for them, and re-layouts: 50.5 us -> none  [the longest x1 36.6 us: shards(): grad_route = (jnp.einsum('emf,edf->emd', grad_first, w_gate, preferred_el...]
    dot_general x6 -> x12, matrix products: 42.7 us -> 87.6 us  [the longest x2 29.8 us: gathered_shards(): jnp.dot(second.astype(jnp.bfloat16), w_up[e].T, preferred_element_type=jn...]
    all_gather x0 -> x1, blocking collectives: none -> 39.1 us  [gathered_shards(): all_gates = lax.all_gather(dense, axes, axis=0, tiled=True)]
    all_to_all x3 -> x0, starting transfers between devices: 27.3 us -> none  [the longest x1 14.4 us: shards(): lax.all_to_all(send_grads.reshape(flat_shape), ('gx', 'gy'), split_axis=1...]
  transfers between devices with their start and end apart: 3 -> 3, of which waited for: 3 -> 3; matrix products, arithmetic and copies ran while one was open for 15% -> 6% of each run, Pallas kernels for 0% -> 0%
where the time goes in v1:
time: 346 us
  waiting for transfers between devices  201 us (58%)
  matrix products  87.6 us (25%)
  blocking collectives  39.1 us (11%)
  between operations  14 us (4%)
    reduce_scatter x1, waiting for transfers between devices, gathered_shards(): lax.psum_scatter(total.astype(jnp.bfloat16), axes, scatter_dimension=0, t...  87.6 us
    all_gather x1, waiting for transfers between devices, gathered_shards(): grads = lax.all_gather(grad_out, axes, axis=0, tiled=True)  69.4 us
    all_gather x1, waiting for transfers between devices, gathered_shards(): inputs = lax.all_gather(tokens, axes, axis=0, tiled=True)  42.8 us
    all_gather x1, blocking collectives, gathered_shards(): all_gates = lax.all_gather(dense, axes, axis=0, tiled=True)  39.1 us
    dot_general x2, matrix products, gathered_shards(): jnp.dot(second.astype(jnp.bfloat16), w_up[e].T, preferred_element_type=jn...  29.8 us
    dot_general x2, matrix products, gathered_shards(): jnp.dot(first.astype(jnp.bfloat16), w_gate[e].T, preferred_element_type=j...  17.3 us
    dot_general x2, matrix products, gathered_shards(): jnp.dot(hidden.T, routed, preferred_element_type=jnp.float32)  13.8 us
    dot_general x2, matrix products, gathered_shards(): pre_up = jnp.dot(inputs, w_up[e], preferred_element_type=jnp.float32)  9.1 us
  transfers between devices with their start and end apart: 3, of which 3 were waited for; matrix products, arithmetic and copies ran while one was open for 6% of the time, Pallas kernels for 0%

profile of v1, /device:TPU:0, one launch (start us, length us, event | category | flops | bytes accessed | tf_op | source)
XLA Modules:
  0.0 345.7 jit_solution(7287916048845730140)
XLA Ops:
  7.2 0.0 all-gather.5.cloned.1.call-start
  7.2 0.7 all-gather.5.cloned.1.call-update
  7.9 0.0 all-gather.3.cloned.1.call-start
  7.9 0.7 all-gather.3.cloned.1.call-update
  8.6 0.0 reduce-scatter.2.cloned.1.call-start
  8.7 0.7 select_reduce_fusion
  9.4 39.1 %all_gather.9 = f32[2048,32]{0,1:T(8,128)S(1)} all-gather(f32[128,32]{0,1:T(8,128)S(1)} %select_reduce_fusion), channel_id=1, replica_groups=mesh['rep'=2,'gx'=4,'gy'=4] {'gx','gy'}, dimensions={0}, use_global_device_ids=true | all-gather | bytes 278528 | tf_op jit(solution)/shard_map/all_gather | solution.py:77
  48.5 42.8 %all-gather.5.cloned.1.call-done = bf16[2048,2048]{1,0:T(8,128)(2,1)} async-done(((bf16[128,2048]{1,0:T(8,128)(2,1)}), bf16[2048,2048]{1,0:T(8,128)(2,1)}) %all-gather.5.cloned.1.call-update) | async-done | bytes 8388624 | tf_op jit(solution)/shard_map/all_gather | solution.py:78
  91.3 6.0 %fusion.35 = f32[2048,256]{1,0:T(8,128)S(1)} fusion(bf16[2048,2048]{1,0:T(8,128)(2,1)} %all-gather.5.cloned.1.call-done, bf16[2,2048,256]{2,1,0:T(8,128)(2,1)} %param.11), kind=kOutput, calls=%fused_computation.35 | convolution fusion | flops 2147483648 | bytes 11534336 | tf_op jit(solution)/shard_map/dot_general | solution.py:86
  97.3 69.4 %all-gather.3.cloned.1.call-done = bf16[2048,2048]{1,0:T(8,128)(2,1)} async-done(((bf16[128,2048]{1,0:T(8,128)(2,1)}), bf16[2048,2048]{1,0:T(8,128)(2,1)}) %all-gather.3.cloned.1.call-update) | async-done | bytes 8388624 | tf_op jit(solution)/shard_map/all_gather | solution.py:79
  166.7 6.4 %fusion.8 = f32[2048,256]{1,0:T(8,128)S(1)} fusion(bf16[2048,2048]{1,0:T(8,128)(2,1)} %all-gather.3.cloned.1.call-done, f32[2048]{0:T(1024)S(1)} %bitcast.38, bf16[2,256,2048]{2,1,0:T(8,128)(2,1)} %param.13), kind=kOutput, calls=%fused_computation.8 | convolution fusion | flops 2160066560 | bytes 11542528 | tf_op jit(solution)/shard_map/dot_general | solution.py:91
  173.1 0.0 slice-start.3
  173.1 8.1 %fusion.25 = f32[2048,2048]{1,0:T(8,128)} fusion(f32[2048,256]{1,0:T(8,128)S(1)} %fusion.8, bf16[2,2048,256]{2,1,0:T(8,128)(2,1)S(1)} %copy-done.6, f32[2048,256]{1,0:T(8,128)S(1)} %fusion.35), kind=kOutput, calls=%fused_computation.25 | convolution fusion | flops 2150629376 | bytes 22020096 | tf_op jit(solution)/shard_map/dot_general | solution.py:97
  181.3 2.4 fusion.38
  183.7 0.0 copy-done.7
  183.7 0.0 copy-start.5
  183.7 8.7 %fusion.24 = f32[2048,2048]{1,0:T(8,128)} fusion(f32[2048,256]{1,0:T(8,128)S(1)} %fusion.35, f32[2048,256]{1,0:T(8,128)S(1)} %fusion.8, f32[2048,256]{1,0:T(8,128)S(1)} %fusion.38, bf16[2,2048,256]{2,1,0:T(8,128)(2,1)S(1)} %copy-done.7), kind=kOutput, calls=%fused_computation.24 | convolution fusion | flops 2152726528 | bytes 24117248 | tf_op jit(solution)/shard_map/dot_general | solution.py:94
  192.4 2.6 fusion.28
  195.1 0.0 slice-start.1
  195.1 0.0 copy-start.8
  195.1 6.6 %fusion.31 = f32[2048,256]{1,0:T(8,128)S(1)} fusion(bf16[2048,2048]{1,0:T(8,128)(2,1)} %all-gather.5.cloned.1.call-done, bf16[2,2048,256]{2,1,0:T(8,128)(2,1)S(1)} %copy-done.6), kind=kOutput, calls=%fused_computation.31 | convolution fusion | flops 2147483648 | bytes 11534336 | tf_op jit(solution)/shard_map/dot_general | solution.py:87
  201.8 0.0 copy-start.3
  201.8 2.6 fusion.4
  204.5 0.0 copy-start.2
  204.5 1.3 copy-done.2
  205.8 8.6 %fusion.26 = f32[2048,2048]{1,0:T(8,128)} fusion(f32[2048,256]{1,0:T(8,128)S(1)} %fusion.28, f32[2048,256]{1,0:T(8,128)S(1)} %fusion.4, f32[2048,256]{1,0:T(8,128)S(1)} %fusion.31, bf16[2,2048,256]{2,1,0:T(8,128)(2,1)S(1)} %copy-done.7), kind=kOutput, calls=%fused_computation.26 | convolution fusion | flops 2152726528 | bytes 24117248 | tf_op jit(solution)/shard_map/dot_general | solution.py:94
  214.4 21.7 %add_convert_fusion = bf16[2048,2048]{1,0:T(8,128)(2,1)} fusion(f32[2048,2048]{1,0:T(8,128)} %fusion.26, f32[2048,2048]{1,0:T(8,128)} %fusion.24, f32[2048,2048]{1,0:T(8,128)} %fusion.25, f32[2048,256]{1,0:T(8,128)} %copy-done.2, bf16[2,2048,256]{2,1,0:T(8,128)(2,1)} %param.12, f32[2048,256]{1,0:T(8,128)} %copy-done), kind=kOutput, calls=%fused_computation.4 | convolution fusion | flops 2167406592 | bytes 63963136 | tf_op jit(solution)/shard_map/dot_general | solution.py:97
  236.1 0.0 reduce-scatter.2.cloned.1.call-update
  236.1 7.0 %fusion.19 = bf16[1,256,2048]{2,1,0:T(8,128)(2,1)S(1)} fusion(bf16[2048,2048]{1,0:T(8,128)(2,1)} %all-gather.3.cloned.1.call-done, f32[2048]{0:T(1024)S(1)} %bitcast.39, f32[2048,256]{1,0:T(8,128)} %copy-done.5, f32[2048,256]{1,0:T(8,128)S(1)} %fusion.35), kind=kOutput, calls=%fused_computation.12 | convolution fusion | flops 2163736576 | bytes 13639680 | tf_op jit(solution)/shard_map/dot_general | solution.py:101
  243.2 6.8 %fusion.16 = bf16[1,256,2048]{2,1,0:T(8,128)(2,1)S(1)} fusion(bf16[2048,2048]{1,0:T(8,128)(2,1)} %all-gather.3.cloned.1.call-done, f32[2048]{0:T(1024)S(1)} %bitcast.37, f32[2048,256]{1,0:T(8,128)S(1)} %copy-done.4, f32[2048,256]{1,0:T(8,128)S(1)} %copy-done.1), kind=kOutput, calls=%fused_computation.11 | convolution fusion | flops 2163736576 | bytes 13639680 | tf_op jit(solution)/shard_map/dot_general | solution.py:101
  250.0 1.5 pad_maximum_fusion
  251.5 87.6 %reduce-scatter.2.cloned.1.call-done = bf16[128,2048]{1,0:T(8,128)(2,1)} async-done(((bf16[2048,2048]{1,0:T(8,128)(2,1)}), bf16[128,2048]{1,0:T(8,128)(2,1)}) %reduce-scatter.2.cloned.1.call-update) | async-done | bytes 524304 | tf_op jit(solution)/shard_map/reduce_scatter | solution.py:103
  (21 shorter events, 0.1 us)
Async XLA Ops:
  7.2 84.2 %all-gather.5.cloned.1.call-start = ((), (), s32[]{:S(2)}) async-start(), calls=%async_computation.2 | async-start | bytes 8912896 | tf_op jit(solution)/shard_map/all_gather | solution.py:78
  7.9 158.8 %all-gather.3.cloned.1.call-start = ((), (), s32[]{:S(2)}) async-start(), calls=%async_computation.1 | async-start | bytes 8912896 | tf_op jit(solution)/shard_map/all_gather | solution.py:79
  8.6 330.5 %reduce-scatter.2.cloned.1.call-start = ((), (), s32[]{:S(2)}) async-start(), calls=%async_computation.3 | async-start | bytes 8912896 | tf_op jit(solution)/shard_map/reduce_scatter | solution.py:103
  166.7 6.4 %copy-start.6 = (bf16[2,2048,256]{2,1,0:T(8,128)(2,1)S(1)}, bf16[2,2048,256]{2,1,0:T(8,128)(2,1)}, u32[]{:S(2)}) copy-start(bf16[2,2048,256]{2,1,0:T(8,128)(2,1)} %param.12) | copy-start | bytes 6291460
  166.7 14.5 %slice-start.2 = ((s8[8388608]{0:T(1024)(128)(4,1)}), s8[4194304]{0:T(1024)(128)(4,1)S(1)}, s32[]{:S(2)}) async-start(s8[8388608]{0:T(1024)(128)(4,1)} %bitcast.42), calls=%async_computation.6 | async-start | bytes 8388608
  173.1 8.2 %slice-start.3 = ((s8[8388608]{0:T(1024)(128)(4,1)}), s8[4194304]{0:T(1024)(128)(4,1)S(1)}, s32[]{:S(2)}) async-start(s8[8388608]{0:T(1024)(128)(4,1)} %bitcast.42), calls=%async_computation.7 | async-start | bytes 8388608
  181.3 2.5 copy-start.7
  183.7 8.7 %copy-start.5 = (f32[2048,256]{1,0:T(8,128)}, f32[2048,256]{1,0:T(8,128)S(1)}, u32[]{:S(2)}) copy-start(f32[2048,256]{1,0:T(8,128)S(1)} %fusion.38) | copy-start | bytes 6291460
  192.4 9.4 %slice-start = ((s8[8388608]{0:T(1024)(128)(4,1)}), s8[4194304]{0:T(1024)(128)(4,1)S(1)}, s32[]{:S(2)}) async-start(s8[8388608]{0:T(1024)(128)(4,1)} %bitcast.40), calls=%async_computation.4 | async-start | bytes 8388608
  195.1 9.4 %copy-start = (f32[2048,256]{1,0:T(8,128)}, f32[2048,256]{1,0:T(8,128)S(1)}, u32[]{:S(2)}) copy-start(f32[2048,256]{1,0:T(8,128)S(1)} %fusion.28) | copy-start | bytes 6291460
  195.1 6.7 %slice-start.1 = ((s8[8388608]{0:T(1024)(128)(4,1)}), s8[4194304]{0:T(1024)(128)(4,1)S(1)}, s32[]{:S(2)}) async-start(s8[8388608]{0:T(1024)(128)(4,1)} %bitcast.40), calls=%async_computation.5 | async-start | bytes 8388608
  195.1 6.7 %copy-start.8 = (bf16[2,256,2048]{2,1,0:T(8,128)(2,1)S(1)}, bf16[2,256,2048]{2,1,0:T(8,128)(2,1)}, u32[]{:S(2)}) copy-start(bf16[2,256,2048]{2,1,0:T(8,128)(2,1)} %param.13) | copy-start | bytes 6291460
  201.8 2.7 copy-start.3
  204.5 1.3 copy-start.2
  236.1 7.0 %copy-start.1 = (f32[2048,256]{1,0:T(8,128)S(1)}, f32[2048,256]{1,0:T(8,128)}, u32[]{:S(2)}) copy-start(f32[2048,256]{1,0:T(8,128)} %copy-done) | copy-start | bytes 6291460
  236.1 7.0 %copy-start.4 = (f32[2048,256]{1,0:T(8,128)S(1)}, f32[2048,256]{1,0:T(8,128)}, u32[]{:S(2)}) copy-start(f32[2048,256]{1,0:T(8,128)} %copy-done.3) | copy-start | bytes 6291460
Sparse Core Ops, SparseCore 0:
  10.2 81.0 all-gather.4
  93.5 73.1 all-gather.2
  236.2 102.8 reduce-scatter.1

commit v2 on v0

--- a/solution.py
+++ b/solution.py
@@ -1,10 +1,16 @@
 import jax
 import jax.numpy as jnp
 from jax import lax
+from jax.experimental import pallas as pl
+from jax.experimental.pallas import tpu as pltpu
 from jax.sharding import PartitionSpec as P
 
 
-def shards(tokens, grad_out, route_ids, gate_weights, w_gate, w_up, w_down):
+LINE = 4
+TILE = 512
+
+
+def routed_shards(tokens, grad_out, route_ids, gate_weights, w_gate, w_up, w_down):
     token_count = tokens.shape[0]
     model_width = tokens.shape[1]
     fanout = route_ids.shape[1]
@@ -67,6 +73,323 @@
     return (grad_tokens, grad_down)
 
 
+def fused_kernel(
+    tok_in, grd_in, gat_in, wg_in, wu_in, wd_in, gt_out, gd_out,
+    tok, grd, gat, wg, wu, wd, part, core_in, y_in, z_in, down, g_first, g_second, hid, acc,
+    local_sem, w_sem, send_sem, recv_sem, a_send, a_recv, b_send, b_recv, c_send, c_recv,
+):
+    gx, z = lax.axis_index("gx"), lax.axis_index("gy")
+    y, c = gx // 2, gx % 2
+    me = gx * LINE + z
+    nbr = (
+        {"gx": gx, "gy": z + 1},
+        {"gx": gx, "gy": z - 1},
+        {"gx": (1 - y) * 2 + c, "gy": z},
+        {"gx": y * 2 + 1 - c, "gy": z},
+    )
+    bufs = (tok, grd, gat)
+    own = y * LINE + z
+    high = z // 2
+    edge = z + high * (3 - 2 * z)
+
+    def place(r):
+        o = r + edge * (1 - r // 2) * (1 - 2 * (r % 2))
+        return o + high * (3 - 2 * o)
+
+    def hop(k, u, cc, d):
+        return pltpu.make_async_remote_copy(
+            src_ref=bufs[k].at[u, cc],
+            dst_ref=bufs[k].at[u, cc],
+            send_sem=send_sem.at[k, u, d],
+            recv_sem=recv_sem.at[k, u, cc],
+            device_id=nbr[d],
+            device_id_type=pl.DeviceIdType.MESH,
+        )
+
+    def each_hop(k, zu, act):
+        u = y * LINE + zu
+
+        @pl.when((zu <= z) & (z < LINE - 1))
+        def _():
+            act(hop(k, u, c, 0))
+
+        @pl.when((zu >= z) & (z > 0))
+        def _():
+            act(hop(k, u, c, 1))
+
+        act(hop(k, u, c, 2))
+        act(hop(k, u, c, 3))
+
+    def start(copy):
+        copy.start()
+
+    def done(copy):
+        copy.wait_send()
+
+    locals_ = [
+        pltpu.make_async_copy(src, buf.at[own, c], local_sem.at[k])
+        for k, (src, buf) in enumerate(((tok_in, tok), (grd_in, grd), (gat_in, gat)))
+    ]
+    weights = [
+        pltpu.make_async_copy(src, dst, w_sem.at[k])
+        for k, (src, dst) in enumerate(((wg_in, wg), (wu_in, wu), (wd_in, wd)))
+    ]
+    for copy in locals_ + weights:
+        copy.start()
+
+    barrier = pltpu.get_barrier_semaphore()
+
+    def greet(d):
+        pl.semaphore_signal(
+            barrier, inc=1, device_id=nbr[d], device_id_type=pl.DeviceIdType.MESH
+        )
+
+    pl.when(z < LINE - 1)(lambda: greet(0))
+    pl.when(z > 0)(lambda: greet(1))
+    greet(2)
+    greet(3)
+    inside = (z + LINE - 1) // LINE * ((2 * LINE - 2 - z) // LINE)
+    pl.semaphore_wait(barrier, 3 + inside)
+
+    for copy in locals_:
+        copy.wait()
+    for k in (0, 2, 1):
+        each_hop(k, z, start)
+    down[...] = jnp.zeros_like(down)
+    for copy in weights:
+        copy.wait()
+
+    def core_copy(u):
+        return pltpu.make_async_remote_copy(
+            src_ref=part.at[u, 1 - c],
+            dst_ref=core_in.at[u],
+            send_sem=a_send.at[u],
+            recv_sem=a_recv.at[u],
+            device_id=nbr[3],
+            device_id_type=pl.DeviceIdType.MESH,
+        )
+
+    def y_copy(zu):
+        return pltpu.make_async_remote_copy(
+            src_ref=part.at[(1 - y) * LINE + zu, c],
+            dst_ref=y_in.at[zu],
+            send_sem=b_send.at[zu],
+            recv_sem=b_recv.at[zu],
+            device_id=nbr[2],
+            device_id_type=pl.DeviceIdType.MESH,
+        )
+
+    def z_copy(zu, d):
+        return pltpu.make_async_remote_copy(
+            src_ref=part.at[y * LINE + zu, c],
+            dst_ref=z_in.at[d, zu],
+            send_sem=c_send.at[zu],
+            recv_sem=c_recv.at[d, zu],
+            device_id=nbr[d],
+            device_id_type=pl.DeviceIdType.MESH,
+        )
+
+    def compute(u):
+        rows, width, f = 2 * tok.shape[2], tok.shape[3], wg.shape[2]
+
+        def expert(e, _):
+            x = tok[u].reshape(rows, width)
+            g = grd[u].reshape(rows, width)
+            pg = jnp.dot(x, wg[e], preferred_element_type=jnp.float32)
+            pu = jnp.dot(x, wu[e], preferred_element_type=jnp.float32)
+            gh = lax.dot_general(
+                g, wd[e], (((1,), (1,)), ((), ())), preferred_element_type=jnp.float32
+            )
+            row = me * wg.shape[0] + e
+            cols = []
+            for cc in range(2):
+                line = gat[u, cc, pl.ds(row, 1), :]
+                t = jnp.broadcast_to(line, (line.shape[1], line.shape[1])).T
+                cols.append(jnp.concatenate([t] * (f // t.shape[1]), axis=1))
+            gate = jnp.concatenate(cols, axis=0)
+            sigma = jax.nn.sigmoid(pg)
+            silu_val = pg * sigma
+            hid[e] = (gate * (silu_val * pu)).T.astype(jnp.bfloat16)
+            gh = gh * gate
+            g_first[e] = (gh * pu * sigma * (1.0 + pg * (1.0 - sigma))).astype(jnp.bfloat16)
+            g_second[e] = (gh * silu_val).astype(jnp.bfloat16)
+            return 0
+
+        lax.fori_loop(0, wg.shape[0], expert, 0)
+
+        def columns(n, _):
+            cs = pl.ds(pl.multiple_of(n * TILE, TILE), TILE)
+            g = grd[u, :, :, cs].reshape(rows, TILE)
+            total = None
+            for e in range(wg.shape[0]):
+                for a, w in ((g_first, wg), (g_second, wu)):
+                    t = lax.dot_general(
+                        a[e], w[e, cs, :], (((1,), (1,)), ((), ())),
+                        preferred_element_type=jnp.float32,
+                    )
+                    total = t if total is None else total + t
+                down[e, :, cs] += jnp.dot(hid[e], g, preferred_element_type=jnp.float32)
+            half = rows // 2
+            part[u, 0, :, cs] = total[:half].astype(jnp.bfloat16)
+            part[u, 1, :, cs] = total[half:].astype(jnp.bfloat16)
+            return 0
+
+        lax.fori_loop(0, width // TILE, columns, 0)
+        core_copy(u).start()
+
+    def round_(r, _):
+        for group in ((0, 2), (1,)):
+            @pl.when((r > 0) & (r < LINE))
+            def _():
+                for k in group:
+                    hop(k, y * LINE + place(r), c, 3).wait_recv()
+                    each_hop(k, place(r), start)
+
+            @pl.when(r > 0)
+            def _():
+                for k in group:
+                    copy = hop(k, (1 - y) * LINE + place(r - 1), c, 3)
+                    copy.wait_recv()
+                    copy.start()
+
+        def half(h, _):
+            @pl.when((r - h >= 0) & (r - h < LINE))
+            def _():
+                u = (y + h * (1 - 2 * y)) * LINE + place(r - h)
+                for k in range(3):
+                    hop(k, u, 1 - c, 3).wait_recv()
+                compute(u)
+            return 0
+
+        lax.fori_loop(0, 2, half, 0)
+        return 0
+
+    lax.fori_loop(0, LINE + 1, round_, 0)
+
+    def send_y(j, _):
+        zu = place(LINE - 1 - j)
+        v = (1 - y) * LINE + zu
+        core_copy(v).wait_recv()
+        part[v, c] = (part[v, c].astype(jnp.float32) + core_in[v].astype(jnp.float32)).astype(
+            jnp.bfloat16
+        )
+        y_copy(zu).start()
+        return 0
+
+    lax.fori_loop(0, LINE, send_y, 0)
+    gd_out[...] = down[...].astype(gd_out.dtype)
+
+    def send_z(j, _):
+        zu = place(LINE - 1 - j)
+        u = y * LINE + zu
+        core_copy(u).wait_recv()
+        acc[...] = part[u, c].astype(jnp.float32) + core_in[u].astype(jnp.float32)
+        y_copy(zu).wait_recv()
+        acc[...] += y_in[zu].astype(jnp.float32)
+
+        @pl.when((zu >= z) & (z > 0))
+        def _():
+            z_copy(zu, 0).wait_recv()
+            acc[...] += z_in[0, zu].astype(jnp.float32)
+
+        @pl.when((zu <= z) & (z < LINE - 1))
+        def _():
+            z_copy(zu, 1).wait_recv()
+            acc[...] += z_in[1, zu].astype(jnp.float32)
+
+        @pl.when(zu == z)
+        def _():
+            gt_out[...] = acc[...].astype(gt_out.dtype)
+
+        @pl.when(zu > z)
+        def _():
+            part[u, c] = acc[...].astype(jnp.bfloat16)
+            z_copy(zu, 0).start()
+
+        @pl.when(zu < z)
+        def _():
+            part[u, c] = acc[...].astype(jnp.bfloat16)
+            z_copy(zu, 1).start()
+        return 0
+
+    lax.fori_loop(0, LINE, send_z, 0)
+
+    def drain(zu, _):
+        for k in range(3):
+            each_hop(k, zu, done)
+            hop(k, (1 - y) * LINE + zu, c, 3).wait_send()
+        core_copy(zu).wait_send()
+        core_copy(LINE + zu).wait_send()
+        y_copy(zu).wait_send()
+        pl.when(zu > z)(lambda: z_copy(zu, 0).wait_send())
+        pl.when(zu < z)(lambda: z_copy(zu, 1).wait_send())
+        return 0
+
+    lax.fori_loop(0, LINE, drain, 0)
+
+
+def fused_shards(tokens, grad_out, route_ids, gate_weights, w_gate, w_up, w_down):
+    rows, width = tokens.shape
+    local_experts, _, ff = w_gate.shape
+    experts = local_experts * lax.axis_size("gx") * lax.axis_size("gy")
+    units = 2 * LINE
+    names = jnp.arange(experts, dtype=jnp.int32)[None, :, None]
+    dense = jnp.sum(
+        jnp.where(route_ids.T[:, None, :] == names, gate_weights.T[:, None, :], 0.0), axis=0
+    )
+    bf16, f32 = jnp.bfloat16, jnp.float32
+    dma = pltpu.SemaphoreType.DMA
+    return pl.pallas_call(
+        fused_kernel,
+        out_shape=(
+            jax.ShapeDtypeStruct((rows, width), bf16),
+            jax.ShapeDtypeStruct((local_experts, ff, width), bf16),
+        ),
+        in_specs=[pl.BlockSpec(memory_space=pl.ANY)] * 6,
+        out_specs=[pl.BlockSpec(memory_space=pltpu.VMEM)] * 2,
+        scratch_shapes=[
+            pltpu.VMEM((units, 2, rows, width), bf16),
+            pltpu.VMEM((units, 2, rows, width), bf16),
+            pltpu.VMEM((units, 2, experts, rows), f32),
+            pltpu.VMEM(w_gate.shape, bf16),
+            pltpu.VMEM(w_up.shape, bf16),
+            pltpu.VMEM(w_down.shape, bf16),
+            pltpu.VMEM((units, 2, rows, width), bf16),
+            pltpu.VMEM((units, rows, width), bf16),
+            pltpu.VMEM((LINE, rows, width), bf16),
+            pltpu.VMEM((2, LINE, rows, width), bf16),
+            pltpu.VMEM((local_experts, ff, width), f32),
+            pltpu.VMEM((local_experts, 2 * rows, ff), bf16),
+            pltpu.VMEM((local_experts, 2 * rows, ff), bf16),
+            pltpu.VMEM((local_experts, ff, 2 * rows), bf16),
+            pltpu.VMEM((rows, width), f32),
+            dma((3,)),
+            dma((3,)),
+            dma((3, units, 4)),
+            dma((3, units, 2)),
+            dma((units,)),
+            dma((units,)),
+            dma((LINE,)),
+            dma((LINE,)),
+            dma((LINE,)),
+            dma((2, LINE)),
+        ],
+        compiler_params=pltpu.CompilerParams(
+            collective_id=0, has_side_effects=True, vmem_limit_bytes=60 * 1024 * 1024
+        ),
+    )(tokens, grad_out, dense, w_gate, w_up, w_down)
+
+
+def shards(*args):
+    tokens, route_ids, w_gate = args[0], args[2], args[4]
+    outer, inner = lax.axis_size("gx"), lax.axis_size("gy")
+    experts = w_gate.shape[0] * outer * inner
+    fits = tokens.shape[0] == 128 and w_gate.shape == (2, 2048, 256)
+    if outer == 4 and inner == LINE and fits and experts <= 4 * route_ids.shape[1]:
+        return fused_shards(*args)
+    return routed_shards(*args)
+
+
 def solution(mesh):
     placed = (
         P(("rep", "gx", "gy"), None),

time: 657 us -> 168 us (0.26); the launches traced: 647 us -> 167 us
  waiting for transfers between devices: 337 us -> 0 us
  local copies, waits for them, and re-layouts: 201 us -> 5.04 us
  Pallas kernels: 0 us -> 160 us
  matrix products: 42.7 us -> 0 us
  other arithmetic: 38.3 us -> 1.34 us
  starting transfers between devices: 27.3 us -> 0 us
    all_to_all x3 -> x0, waiting for transfers between devices: 337 us -> none  [the longest x1 135 us: shards(): lax.all_to_all(grad_route.reshape(flat_shape), ('gx', 'gy'), split_axis=1...]
    pallas_call x0 -> x1, Pallas kernels: none -> 160 us  [fused_shards(): pl.pallas_call(fused_kernel, out_shape=(jax.ShapeDtypeStruct((rows, width...]
    reshape x7 -> x0, local copies, waits for them, and re-layouts: 85.6 us -> none  [the longest x2 33.4 us: shards(): send_grads.reshape(flat_shape)]
    convert_element_type x2 -> x0, local copies, waits for them, and re-layouts: 50.5 us -> none  [the longest x1 36.6 us: shards(): grad_route = (jnp.einsum('emf,edf->emd', grad_first, w_gate, preferred_el...]
    dot_general x6 -> x0, matrix products: 42.7 us -> none  [the longest x1 9.6 us: shards(): jnp.einsum('emf,emd->efd', hidden, routed, preferred_element_type=jnp.flo...]
    all_to_all x3 -> x0, starting transfers between devices: 27.3 us -> none  [the longest x1 14.4 us: shards(): lax.all_to_all(send_grads.reshape(flat_shape), ('gx', 'gy'), split_axis=1...]
    gather x2 -> x0, local copies, waits for them, and re-layouts: 24.5 us -> none  [shards(): picked = returned.reshape(buffer_rows, model_width)[position]]
    scatter x1 -> x0, other arithmetic: 20.5 us -> none  [shards(): jnp.zeros((buffer_rows, model_width), jnp.bfloat16).at[position].set(scaled)]
  transfers between devices with their start and end apart: 3 -> 0, of which waited for: 3 -> 0; matrix products, arithmetic and copies ran while one was open for 15% -> 0% of each run, Pallas kernels for 0% -> 0%
where the time goes in v2:
time: 168 us; the launch traced here: 167 us
  Pallas kernels  160 us (95%)
  local copies, waits for them, and re-layouts  5.04 us (3%)
    pallas_call x1, Pallas kernels, fused_shards(): pl.pallas_call(fused_kernel, out_shape=(jax.ShapeDtypeStruct((rows, width...  160 us
    unnamed x2, local copies, waits for them, and re-layouts  5.04 us

profile of v2, /device:TPU:0, one launch (start us, length us, event | category | flops | bytes accessed | tf_op | source)
XLA Modules:
  0.0 167.3 jit_solution(12391287356720729138)
XLA Ops:
  0.6 1.3 select_reduce_fusion.gat_in
  2.0 160.3 %shard_map.86 = (bf16[128,2048]{1,0:T(8,128)(2,1)}, bf16[2,256,2048]{2,1,0:T(8,128)(2,1)}) custom-call(bf16[128,2048]{1,0:T(8,128)(2,1)} %tok_in.1, bf16[128,2048]{1,0:T(8,128)(2,1)} %grd_in.1, f32[32,128]{1,0:T(8,128)} %select_reduce_fusion.gat_in, bf16[2,2048,256]{2,1,0:T(8,128)(2,1)} %wg_in.1, bf16[2,2048,256]{2,1,0:T(8,128)(2,1)} %wu_in.1, ...), custom_call_target="tpu_custom_call" | custom-call | tf_op jit(solution)/shard_map/pallas_call | solution.py:342
  162.3 1.9 %copy.11 = bf16[128,2048]{1,0:T(8,128)(2,1)} copy(bf16[128,2048]{1,0:T(8,128)(2,1)} %get-tuple-element.4) | data formatting | bytes 1048576
  164.2 3.2 %copy.12 = bf16[2,256,2048]{2,1,0:T(8,128)(2,1)} copy(bf16[2,256,2048]{2,1,0:T(8,128)(2,1)} %get-tuple-element.5) | data formatting | bytes 4194304

commit v3 on v2

--- a/solution.py
+++ b/solution.py
@@ -8,6 +8,7 @@
 
 LINE = 4
 TILE = 512
+PARTS = 2
 
 
 def routed_shards(tokens, grad_out, route_ids, gate_weights, w_gate, w_up, w_down):
@@ -87,7 +88,9 @@
         {"gx": (1 - y) * 2 + c, "gy": z},
         {"gx": y * 2 + 1 - c, "gy": z},
     )
-    bufs = (tok, grd, gat)
+    rows = tok.shape[2]
+    kinds = 1 + 2 * PARTS
+    half_rows = rows // 2
     own = y * LINE + z
     high = z // 2
     edge = z + high * (3 - 2 * z)
@@ -96,10 +99,16 @@
         o = r + edge * (1 - r // 2) * (1 - 2 * (r % 2))
         return o + high * (3 - 2 * o)
 
+    def piece(k, u, cc):
+        if k == 0:
+            return gat.at[u, cc]
+        size = rows // PARTS
+        return (tok, grd)[(k - 1) // PARTS].at[u, cc, pl.ds((k - 1) % PARTS * size, size)]
+
     def hop(k, u, cc, d):
         return pltpu.make_async_remote_copy(
-            src_ref=bufs[k].at[u, cc],
-            dst_ref=bufs[k].at[u, cc],
+            src_ref=piece(k, u, cc),
+            dst_ref=piece(k, u, cc),
             send_sem=send_sem.at[k, u, d],
             recv_sem=recv_sem.at[k, u, cc],
             device_id=nbr[d],
@@ -153,7 +162,7 @@
 
     for copy in locals_:
         copy.wait()
-    for k in (0, 2, 1):
+    for k in range(kinds):
         each_hop(k, z, start)
     down[...] = jnp.zeros_like(down)
     for copy in weights:
@@ -169,22 +178,25 @@
             device_id_type=pl.DeviceIdType.MESH,
         )
 
-    def y_copy(zu):
+    def span(h):
+        return pl.ds(pl.multiple_of(h * half_rows, half_rows), half_rows)
+
+    def y_copy(zu, h):
         return pltpu.make_async_remote_copy(
-            src_ref=part.at[(1 - y) * LINE + zu, c],
-            dst_ref=y_in.at[zu],
-            send_sem=b_send.at[zu],
-            recv_sem=b_recv.at[zu],
+            src_ref=part.at[(1 - y) * LINE + zu, c, span(h)],
+            dst_ref=y_in.at[zu, span(h)],
+            send_sem=b_send.at[zu, h],
+            recv_sem=b_recv.at[zu, h],
             device_id=nbr[2],
             device_id_type=pl.DeviceIdType.MESH,
         )
 
-    def z_copy(zu, d):
+    def z_copy(zu, h, d):
         return pltpu.make_async_remote_copy(
-            src_ref=part.at[y * LINE + zu, c],
-            dst_ref=z_in.at[d, zu],
-            send_sem=c_send.at[zu],
-            recv_sem=c_recv.at[d, zu],
+            src_ref=part.at[y * LINE + zu, c, span(h)],
+            dst_ref=z_in.at[d, zu, span(h)],
+            send_sem=c_send.at[zu, h],
+            recv_sem=c_recv.at[d, zu, h],
             device_id=nbr[d],
             device_id_type=pl.DeviceIdType.MESH,
         )
@@ -237,26 +249,47 @@
         lax.fori_loop(0, width // TILE, columns, 0)
         core_copy(u).start()
 
+    def turn(j):
+        return place((1 - j // 2) * (2 + j) + j // 2 * (3 - j))
+
+    def send_y(j, _):
+        zu = turn(j)
+        v = (1 - y) * LINE + zu
+        core_copy(v).wait_recv()
+
+        def one(h, _):
+            part[v, c, span(h)] = (
+                part[v, c, span(h)].astype(jnp.float32)
+                + core_in[v, span(h)].astype(jnp.float32)
+            ).astype(jnp.bfloat16)
+            y_copy(zu, h).start()
+            return 0
+
+        lax.fori_loop(0, 2, one, 0)
+        return 0
+
     def round_(r, _):
-        for group in ((0, 2), (1,)):
+        for k in range(kinds):
             @pl.when((r > 0) & (r < LINE))
             def _():
-                for k in group:
-                    hop(k, y * LINE + place(r), c, 3).wait_recv()
-                    each_hop(k, place(r), start)
+                hop(k, y * LINE + place(r), c, 3).wait_recv()
+                each_hop(k, place(r), start)
 
             @pl.when(r > 0)
             def _():
-                for k in group:
-                    copy = hop(k, (1 - y) * LINE + place(r - 1), c, 3)
-                    copy.wait_recv()
-                    copy.start()
+                copy = hop(k, (1 - y) * LINE + place(r - 1), c, 3)
+                copy.wait_recv()
+                copy.start()
+
+        @pl.when(r == LINE)
+        def _():
+            send_y(0, 0)
 
         def half(h, _):
             @pl.when((r - h >= 0) & (r - h < LINE))
             def _():
                 u = (y + h * (1 - 2 * y)) * LINE + place(r - h)
-                for k in range(3):
+                for k in range(kinds):
                     hop(k, u, 1 - c, 3).wait_recv()
                 compute(u)
             return 0
@@ -266,63 +299,60 @@
 
     lax.fori_loop(0, LINE + 1, round_, 0)
 
-    def send_y(j, _):
-        zu = place(LINE - 1 - j)
-        v = (1 - y) * LINE + zu
-        core_copy(v).wait_recv()
-        part[v, c] = (part[v, c].astype(jnp.float32) + core_in[v].astype(jnp.float32)).astype(
-            jnp.bfloat16
-        )
-        y_copy(zu).start()
+    lax.fori_loop(1, LINE, send_y, 0)
+    gd_out[...] = down[...].astype(gd_out.dtype)
+
+    def send_z(i, _):
+        zu, h = turn(i // 2), i % 2
+        u = y * LINE + zu
+
+        @pl.when(h == 0)
+        def _():
+            core_copy(u).wait_recv()
+
+        acc[...] = part[u, c, span(h)].astype(jnp.float32) + core_in[u, span(h)].astype(
+            jnp.float32
+        )
+        y_copy(zu, h).wait_recv()
+        acc[...] += y_in[zu, span(h)].astype(jnp.float32)
+
+        @pl.when((zu >= z) & (z > 0))
+        def _():
+            z_copy(zu, h, 0).wait_recv()
+            acc[...] += z_in[0, zu, span(h)].astype(jnp.float32)
+
+        @pl.when((zu <= z) & (z < LINE - 1))
+        def _():
+            z_copy(zu, h, 1).wait_recv()
+            acc[...] += z_in[1, zu, span(h)].astype(jnp.float32)
+
+        @pl.when(zu == z)
+        def _():
+            gt_out[span(h)] = acc[...].astype(gt_out.dtype)
+
+        @pl.when(zu > z)
+        def _():
+            part[u, c, span(h)] = acc[...].astype(jnp.bfloat16)
+            z_copy(zu, h, 0).start()
+
+        @pl.when(zu < z)
+        def _():
+            part[u, c, span(h)] = acc[...].astype(jnp.bfloat16)
+            z_copy(zu, h, 1).start()
         return 0
 
-    lax.fori_loop(0, LINE, send_y, 0)
-    gd_out[...] = down[...].astype(gd_out.dtype)
-
-    def send_z(j, _):
-        zu = place(LINE - 1 - j)
-        u = y * LINE + zu
-        core_copy(u).wait_recv()
-        acc[...] = part[u, c].astype(jnp.float32) + core_in[u].astype(jnp.float32)
-        y_copy(zu).wait_recv()
-        acc[...] += y_in[zu].astype(jnp.float32)
-
-        @pl.when((zu >= z) & (z > 0))
-        def _():
-            z_copy(zu, 0).wait_recv()
-            acc[...] += z_in[0, zu].astype(jnp.float32)
-
-        @pl.when((zu <= z) & (z < LINE - 1))
-        def _():
-            z_copy(zu, 1).wait_recv()
-            acc[...] += z_in[1, zu].astype(jnp.float32)
-
-        @pl.when(zu == z)
-        def _():
-            gt_out[...] = acc[...].astype(gt_out.dtype)
-
-        @pl.when(zu > z)
-        def _():
-            part[u, c] = acc[...].astype(jnp.bfloat16)
-            z_copy(zu, 0).start()
-
-        @pl.when(zu < z)
-        def _():
-            part[u, c] = acc[...].astype(jnp.bfloat16)
-            z_copy(zu, 1).start()
-        return 0
-
-    lax.fori_loop(0, LINE, send_z, 0)
+    lax.fori_loop(0, 2 * LINE, send_z, 0)
 
     def drain(zu, _):
-        for k in range(3):
+        for k in range(kinds):
             each_hop(k, zu, done)
             hop(k, (1 - y) * LINE + zu, c, 3).wait_send()
         core_copy(zu).wait_send()
         core_copy(LINE + zu).wait_send()
-        y_copy(zu).wait_send()
-        pl.when(zu > z)(lambda: z_copy(zu, 0).wait_send())
-        pl.when(zu < z)(lambda: z_copy(zu, 1).wait_send())
+        for h in range(2):
+            y_copy(zu, h).wait_send()
+            pl.when(zu > z)(lambda: z_copy(zu, h, 0).wait_send())
+            pl.when(zu < z)(lambda: z_copy(zu, h, 1).wait_send())
         return 0
 
     lax.fori_loop(0, LINE, drain, 0)
@@ -362,17 +392,17 @@
             pltpu.VMEM((local_experts, 2 * rows, ff), bf16),
             pltpu.VMEM((local_experts, 2 * rows, ff), bf16),
             pltpu.VMEM((local_experts, ff, 2 * rows), bf16),
-            pltpu.VMEM((rows, width), f32),
+            pltpu.VMEM((rows // 2, width), f32),
             dma((3,)),
             dma((3,)),
-            dma((3, units, 4)),
-            dma((3, units, 2)),
+            dma((1 + 2 * PARTS, units, 4)),
+            dma((1 + 2 * PARTS, units, 2)),
             dma((units,)),
             dma((units,)),
-            dma((LINE,)),
-            dma((LINE,)),
-            dma((LINE,)),
-            dma((2, LINE)),
+            dma((LINE, 2)),
+            dma((LINE, 2)),
+            dma((LINE, 2)),
+            dma((2, LINE, 2)),
         ],
         compiler_params=pltpu.CompilerParams(
             collective_id=0, has_side_effects=True, vmem_limit_bytes=60 * 1024 * 1024

time: 168 us -> 159 us (0.946)
  Pallas kernels: 160 us -> 151 us
    pallas_call x1, Pallas kernels: 160 us -> 151 us  [fused_shards(): pl.pallas_call(fused_kernel, out_shape=(jax.ShapeDtypeStruct((rows, width...]
where the time goes in v3:
time: 159 us; the launch traced here: 158 us
  Pallas kernels  151 us (95%)
  local copies, waits for them, and re-layouts  5.04 us (3%)
    pallas_call x1, Pallas kernels, fused_shards(): pl.pallas_call(fused_kernel, out_shape=(jax.ShapeDtypeStruct((rows, width...  151 us
    unnamed x2, local copies, waits for them, and re-layouts  5.04 us

profile of v3, /device:TPU:0, one launch (start us, length us, event | category | flops | bytes accessed | tf_op | source)
XLA Modules:
  0.0 158.3 jit_solution(4697624665294623808)
XLA Ops:
  0.6 1.3 select_reduce_fusion.gat_in
  2.0 151.3 %shard_map.86 = (bf16[128,2048]{1,0:T(8,128)(2,1)}, bf16[2,256,2048]{2,1,0:T(8,128)(2,1)}) custom-call(bf16[128,2048]{1,0:T(8,128)(2,1)} %tok_in.1, bf16[128,2048]{1,0:T(8,128)(2,1)} %grd_in.1, f32[32,128]{1,0:T(8,128)} %select_reduce_fusion.gat_in, bf16[2,2048,256]{2,1,0:T(8,128)(2,1)} %wg_in.1, bf16[2,2048,256]{2,1,0:T(8,128)(2,1)} %wu_in.1, ...), custom_call_target="tpu_custom_call" | custom-call | tf_op jit(solution)/shard_map/pallas_call | solution.py:372
  153.3 1.9 %copy.11 = bf16[128,2048]{1,0:T(8,128)(2,1)} copy(bf16[128,2048]{1,0:T(8,128)(2,1)} %get-tuple-element.4) | data formatting | bytes 1048576
  155.1 3.2 %copy.12 = bf16[2,256,2048]{2,1,0:T(8,128)(2,1)} copy(bf16[2,256,2048]{2,1,0:T(8,128)(2,1)} %get-tuple-element.5) | data formatting | bytes 4194304

commit v4 on v3

--- a/solution.py
+++ b/solution.py
@@ -9,6 +9,7 @@
 LINE = 4
 TILE = 512
 PARTS = 2
+SUMS = 4
 
 
 def routed_shards(tokens, grad_out, route_ids, gate_weights, w_gate, w_up, w_down):
@@ -90,7 +91,7 @@
     )
     rows = tok.shape[2]
     kinds = 1 + 2 * PARTS
-    half_rows = rows // 2
+    half_rows = rows // SUMS
     own = y * LINE + z
     high = z // 2
     edge = z + high * (3 - 2 * z)
@@ -265,7 +266,7 @@
             y_copy(zu, h).start()
             return 0
 
-        lax.fori_loop(0, 2, one, 0)
+        lax.fori_loop(0, SUMS, one, 0)
         return 0
 
     def round_(r, _):
@@ -303,7 +304,7 @@
     gd_out[...] = down[...].astype(gd_out.dtype)
 
     def send_z(i, _):
-        zu, h = turn(i // 2), i % 2
+        zu, h = turn(i // SUMS), i % SUMS
         u = y * LINE + zu
 
         @pl.when(h == 0)
@@ -341,7 +342,7 @@
             z_copy(zu, h, 1).start()
         return 0
 
-    lax.fori_loop(0, 2 * LINE, send_z, 0)
+    lax.fori_loop(0, SUMS * LINE, send_z, 0)
 
     def drain(zu, _):
         for k in range(kinds):
@@ -349,7 +350,7 @@
             hop(k, (1 - y) * LINE + zu, c, 3).wait_send()
         core_copy(zu).wait_send()
         core_copy(LINE + zu).wait_send()
-        for h in range(2):
+        for h in range(SUMS):
             y_copy(zu, h).wait_send()
             pl.when(zu > z)(lambda: z_copy(zu, h, 0).wait_send())
             pl.when(zu < z)(lambda: z_copy(zu, h, 1).wait_send())
@@ -392,17 +393,17 @@
             pltpu.VMEM((local_experts, 2 * rows, ff), bf16),
             pltpu.VMEM((local_experts, 2 * rows, ff), bf16),
             pltpu.VMEM((local_experts, ff, 2 * rows), bf16),
-            pltpu.VMEM((rows // 2, width), f32),
+            pltpu.VMEM((rows // SUMS, width), f32),
             dma((3,)),
             dma((3,)),
             dma((1 + 2 * PARTS, units, 4)),
             dma((1 + 2 * PARTS, units, 2)),
             dma((units,)),
             dma((units,)),
-            dma((LINE, 2)),
-            dma((LINE, 2)),
-            dma((LINE, 2)),
-            dma((2, LINE, 2)),
+            dma((LINE, SUMS)),
+            dma((LINE, SUMS)),
+            dma((LINE, SUMS)),
+            dma((2, LINE, SUMS)),
         ],
         compiler_params=pltpu.CompilerParams(
             collective_id=0, has_side_effects=True, vmem_limit_bytes=60 * 1024 * 1024

time: 159 us -> 158 us (level)
  no operation moved by 1% of the time
where the time goes in v4:
time: 158 us
  Pallas kernels  151 us (96%)
  local copies, waits for them, and re-layouts  5.04 us (3%)
    pallas_call x1, Pallas kernels, fused_shards(): pl.pallas_call(fused_kernel, out_shape=(jax.ShapeDtypeStruct((rows, width...  151 us
    unnamed x2, local copies, waits for them, and re-layouts  5.04 us

profile of v4, /device:TPU:0, one launch (start us, length us, event | category | flops | bytes accessed | tf_op | source)
XLA Modules:
  0.0 158.1 jit_solution(10530411411846261895)
XLA Ops:
  0.6 1.3 select_reduce_fusion.gat_in
  2.0 151.1 %shard_map.86 = (bf16[128,2048]{1,0:T(8,128)(2,1)}, bf16[2,256,2048]{2,1,0:T(8,128)(2,1)}) custom-call(bf16[128,2048]{1,0:T(8,128)(2,1)} %tok_in.1, bf16[128,2048]{1,0:T(8,128)(2,1)} %grd_in.1, f32[32,128]{1,0:T(8,128)} %select_reduce_fusion.gat_in, bf16[2,2048,256]{2,1,0:T(8,128)(2,1)} %wg_in.1, bf16[2,2048,256]{2,1,0:T(8,128)(2,1)} %wu_in.1, ...), custom_call_target="tpu_custom_call" | custom-call | tf_op jit(solution)/shard_map/pallas_call | solution.py:373
  153.1 1.9 %copy.11 = bf16[128,2048]{1,0:T(8,128)(2,1)} copy(bf16[128,2048]{1,0:T(8,128)(2,1)} %get-tuple-element.4) | data formatting | bytes 1048576
  155.0 3.2 %copy.12 = bf16[2,256,2048]{2,1,0:T(8,128)(2,1)} copy(bf16[2,256,2048]{2,1,0:T(8,128)(2,1)} %get-tuple-element.5) | data formatting | bytes 4194304
